TPU v7x, 256 devices: a whole 4x4x8 slice. The times are simulated.
256 devices in a mesh: gx: 32 (over z, y), gy: 8 (over x, core).
Axes of the slice: x: 4, y: 4, z: 8, core: 2. Of those that a mesh axis runs over, the one named last changes fastest.
Arguments:
- section_start: float32 [5, 64, 256, 1024], P(None, None, 'gx', 'gy'), may hold values from -2 to 8, as said below
- section_now: float32 [5, 64, 256, 1024], P(None, None, 'gx', 'gy'), may hold values from -2 to 8, as said below
- history: bfloat16 [255, 16, 256, 1024], P(None, None, 'gx', 'gy'), may hold values from -9 to 9
Outputs:
- section_next: float32 [5, 64, 256, 1024], P(None, None, 'gx', 'gy')
- triangle: float32 [256, 256], replicated
Inputs may be any that keep to these rules, and one draw needn't show every extreme that they name: `section_start`: component 0 lies in [1, 2], components 1 to 3 are density times a velocity of magnitude at most 1 in each direction, and component 4 is at least the kinetic energy. `section_now`: as section_start.
All inputs are finite; a program needn't handle non-finite values.
Results may differ from a plain program's by a relative error of at most 0.0003.
Values sent between devices are 32-bit elements; how exact they have to be, the bound alone decides.
A program may use at most 128 MiB of HBM per device.

v0:
```python
import functools

import jax
import jax.numpy as jnp
from jax import lax
from jax.experimental import pallas as pl
from jax.experimental.pallas import tpu as pltpu
from jax.sharding import PartitionSpec as P

ZSUB = 4
GAMMA_LESS = 0.4
TIME_STEP = 0.2
VISCOUS = 0.25
MESH = pl.DeviceIdType.MESH
FLUX = 0.25 * TIME_STEP * 0.5
NEAR = 0.25 * TIME_STEP * VISCOUS
OWN = 0.25 - 6.0 * NEAR


def wait_bytes(ref, sem):
    pltpu.make_async_copy(ref, ref, sem).wait()


def pressure_of(q, inverse):
    kinetic = q[1] * q[1] + q[2] * q[2] + q[3] * q[3]
    return GAMMA_LESS * (q[4] - 0.5 * kinetic * inverse)


def plane_of(q):
    inverse = 1.0 / q[0]
    pressure = pressure_of(q, inverse)
    return q, inverse * FLUX, pressure * FLUX, q[4] + pressure


def flux_of(plane, k, sign=None):
    q, scaled, pressure, enthalpy = plane
    if sign is not None:
        scaled, pressure = scaled * sign, pressure * sign
    velocity = q[k] * scaled
    flux = [q[0] * velocity]
    for member in (1, 2, 3):
        term = q[member] * velocity
        flux.append(term + pressure if member == k else term)
    flux.append(enthalpy * velocity)
    return flux


def both_of(plane, k):
    flux = flux_of(plane, k)
    base = [NEAR * value for value in plane[0]]
    return [b + f for b, f in zip(base, flux)], [b - f for b, f in zip(base, flux)]


def edge_of(q, k, sign):
    flux = flux_of(plane_of(q), k, sign)
    return [NEAR * value + f for value, f in zip(q, flux)]


def fold(acc, first, second):
    row = lax.broadcasted_iota(jnp.int32, (256, 128), 0)
    col = lax.broadcasted_iota(jnp.int32, (256, 128), 1)
    total = jnp.zeros((128, 128), jnp.float32)
    for parity in (0, 1):
        pick = (row == 2 * col + parity).astype(jnp.bfloat16)
        for h in (0, 1):
            part = acc[2 * second + h, pl.ds(256 * first + parity, 128, stride=2), :]
            chosen = pick[128 * h : 128 * h + 128]
            for piece in split_of(part):
                total = total + jnp.dot(piece, chosen, preferred_element_type=jnp.float32)
    return total


def split_of(x):
    high = x.astype(jnp.bfloat16)
    rest = x - high.astype(jnp.float32)
    middle = rest.astype(jnp.bfloat16)
    low = (rest - middle.astype(jnp.float32)).astype(jnp.bfloat16)
    return high, middle, low


def section_kernel(
    n_gx, n_gy, planes,
    rows_hbm, now_hbm, start_hbm, hist_hbm, next_hbm, gram_out,
    now, start, result, hist, acc, xhalo, ysend, yhalo,
    packed, rs, rs_extra, ex, gat,
    now_sem, start_sem, hist_sem, out_sem,
    xs, xr, ys, yr, rs_s, rs_r, re_s, re_r, ex_s, ex_r, ag_s, ag_r, ae_s, ae_r,
):
    a, c = lax.axis_index("gx"), lax.axis_index("gy")
    samples = planes // ZSUB
    pairs = hist_hbm.shape[1] // samples
    older = hist_hbm.shape[0]
    load_now = pltpu.make_async_copy(now_hbm, now, now_sem)
    load_start = pltpu.make_async_copy(start_hbm, start, start_sem)
    load_now.start()
    barrier = pltpu.get_barrier_semaphore()

    def greet_gx(d, carry):
        pl.semaphore_signal(barrier, inc=1, device_id=(lax.rem(a + d, n_gx), c), device_id_type=MESH)
        return carry

    def greet_gy(d, carry):
        pl.semaphore_signal(barrier, inc=1, device_id=(a, lax.rem(c + d, n_gy)), device_id_type=MESH)
        return carry

    lax.fori_loop(1, n_gx, greet_gx, 0)
    lax.fori_loop(1, n_gy, greet_gy, 0)
    load_start.start()

    def load_history(z, carry):
        for i in range(pairs):
            pltpu.make_async_copy(
                hist_hbm.at[:, z * pairs + i], hist.at[z * pairs + i, pl.ds(0, older)], hist_sem.at[z]
            ).start()
        return carry

    lax.fori_loop(0, samples, load_history, 0)

    lane = lax.broadcasted_iota(jnp.int32, (8, 128), 1)
    sub = lax.broadcasted_iota(jnp.int32, (8, 128), 0)
    load_now.wait()

    def pack_edges(z, carry):
        mask = lax.rem(lane - 2 * z + 129, 128) < 2
        return tuple(
            jnp.where(mask, pltpu.roll(now[f, z], 2 * z, 1), carry[f]) for f in range(5)
        )

    zero = jnp.zeros((8, 128), jnp.float32)
    edges = lax.fori_loop(0, planes, pack_edges, (zero,) * 5, unroll=4)
    for f in range(5):
        ysend[f] = edges[f]

    pl.semaphore_wait(barrier, n_gx + n_gy - 2)
    up, down = lax.rem(a + 1, n_gx), lax.rem(a + n_gx - 1, n_gx)
    ahead, behind = lax.rem(c + 1, n_gy), lax.rem(c + n_gy - 1, n_gy)

    def to(src, dst, send, recv, where):
        return pltpu.make_async_remote_copy(
            src_ref=src, dst_ref=dst, send_sem=send, recv_sem=recv, device_id=where, device_id_type=MESH
        )

    halos = [
        to(ysend, yhalo.at[0], ys.at[0], yr.at[0], (a, ahead)),
        to(ysend, yhalo.at[1], ys.at[1], yr.at[1], (a, behind)),
        to(rows_hbm.at[:, :, 7], xhalo.at[0], xs.at[0], xr.at[0], (up, c)),
        to(rows_hbm.at[:, :, 0], xhalo.at[1], xs.at[1], xr.at[1], (down, c)),
    ]
    for copy in halos:
        copy.start()
    acc[...] = jnp.zeros_like(acc)
    load_start.wait()
    for copy in halos:
        copy.wait()
    even = lax.rem(lane, 2) == 0
    for f in range(5):
        ysend[f] = jnp.where(even, yhalo[1, f], yhalo[0, f])
    xsign = jnp.where(sub == 7, 1.0, -1.0)
    ysign = jnp.where(lane == 127, 1.0, -1.0)

    def load(z):
        return plane_of([now[f, z] for f in range(5)])

    first = both_of(load(0), 3)[0]

    def step(s, carry):
        below, here = list(carry[:5]), list(carry[5:])
        z0 = s * ZSUB
        plane = load(z0)
        for k in range(ZSUB):
            z = z0 + k
            above = load(jnp.minimum(z + 1, planes - 1))
            up3, down3 = both_of(above, 3)
            p1, n1 = both_of(plane, 1)
            p2, n2 = both_of(plane, 2)
            xq = [jnp.where(sub < 4, xhalo[1, f, z], xhalo[0, f, z]) for f in range(5)]
            xe = edge_of(xq, 1, xsign)
            turn = lax.rem(128 - 2 * z, 128)
            yq = [pltpu.roll(ysend[f], turn, 1) for f in range(5)]
            yq[0] = jnp.where((lane == 0) | (lane == 127), yq[0], 1.0)
            ye = edge_of(yq, 2, ysign)
            fresh = []
            for f in range(5):
                total = below[f] + down3[f]
                total += pltpu.roll(jnp.where(sub == 7, xe[f], p1[f]), 1, 0)
                total += pltpu.roll(jnp.where(sub == 0, xe[f], n1[f]), 7, 0)
                total += pltpu.roll(jnp.where(lane == 127, ye[f], p2[f]), 1, 1)
                total += pltpu.roll(jnp.where(lane == 0, ye[f], n2[f]), 127, 1)
                total += 0.75 * start[f, z] + OWN * plane[0][f]
                result[f, z] = total
                fresh.append(total)
            below, here, plane = here, up3, above
            if k == 0:
                snapshot = pressure_of(fresh, 1.0 / fresh[0]).astype(jnp.bfloat16)
                spot = pl.multiple_of(s * pairs, pairs)
                wait_bytes(hist.at[pl.ds(spot, pairs), pl.ds(0, older)], hist_sem.at[s])
                hist[pl.ds(spot, pairs), older] = snapshot.reshape(pairs, 2, 128)
                block = jnp.concatenate(
                    [hist[spot + i].reshape(2 * older + 2, 128) for i in range(pairs)], axis=1
                )
                for i, j in ((0, 0), (0, 1), (1, 1)):
                    rows, cols = slice(256 * i, 256 * i + 256), slice(256 * j, 256 * j + 256)
                    product = lax.dot_general(
                        block[rows], block[cols], (((1,), (1,)), ((), ())),
                        preferred_element_type=jnp.float32,
                    )
                    acc[2 * j, rows] += product[:, :128]
                    acc[2 * j + 1, rows] += product[:, 128:]
        pltpu.make_async_copy(
            result.at[:, pl.ds(z0, ZSUB)], next_hbm.at[:, pl.ds(z0, ZSUB)], out_sem
        ).start()
        return tuple(below + here)

    lax.fori_loop(0, samples, step, tuple(first + first))

    g00, g01, g11 = fold(acc, 0, 0), fold(acc, 0, 1), fold(acc, 1, 1)
    row = lax.broadcasted_iota(jnp.int32, (128, 128), 0)
    col = lax.broadcasted_iota(jnp.int32, (128, 128), 1)
    mixed = jnp.where(col >= row, g00, g11)
    diagonal = jnp.sum(jnp.where(col == row, g11, 0.0), axis=0, keepdims=True)
    for t in range(16):
        packed[t] = mixed[8 * t : 8 * t + 8]
        packed[16 + t] = g01[8 * t : 8 * t + 8]
    packed[32] = jnp.broadcast_to(diagonal, (8, 128))

    def scatter(d, carry):
        far = lax.rem(a + d, n_gx)
        to(packed.at[far], rs.at[a], rs_s, rs_r, (far, c)).start()
        return carry

    @pl.when(a != 0)
    def _():
        to(packed.at[32], rs_extra.at[a], re_s, re_r, (0, c)).start()

    lax.fori_loop(1, n_gx, scatter, 0)
    rs[a] = packed[a]
    others = pl.ds(0, n_gx - 1)
    wait_bytes(rs.at[others], rs_r)

    def total_of(ref, count):
        total = ref[0]
        for i in range(1, count):
            total = total + ref[i]
        return total

    ex[c, 0] = total_of(rs, n_gx)
    ex[c, 1] = zero

    @pl.when(a == 0)
    def _():
        rs_extra[0] = packed[32]
        wait_bytes(rs_extra.at[others], re_r)
        ex[c, 1] = total_of(rs_extra, n_gx)

    def exchange(d, carry):
        near = lax.rem(c + d, n_gy)
        to(ex.at[c], ex.at[c], ex_s, ex_r, (a, near)).start()
        return carry

    lax.fori_loop(1, n_gy, exchange, 0)
    wait_bytes(ex.at[pl.ds(0, n_gy - 1)], ex_r)
    whole = total_of(ex, n_gy)
    gat[a] = whole[0]

    def spread(d, carry):
        far = lax.rem(a + d, n_gx)
        to(gat.at[a], gat.at[a], ag_s, ag_r, (far, c)).start()
        return carry

    lax.fori_loop(1, n_gx, spread, 0)

    @pl.when(a == 0)
    def _():
        gat[32] = whole[1]

        def spread_extra(d, carry):
            to(gat.at[32], gat.at[32], ae_s, ae_r, (d, c)).start()
            return carry

        lax.fori_loop(1, n_gx, spread_extra, 0)

    wait_bytes(gat.at[others], ag_r)

    @pl.when(a != 0)
    def _():
        wait_bytes(gat.at[32], ae_r)
        wait_bytes(packed.at[32], re_s)

    @pl.when(a == 0)
    def _():
        wait_bytes(gat.at[others], ae_s)

    wait_bytes(rs.at[others], rs_s)
    wait_bytes(ex.at[pl.ds(0, n_gy - 1)], ex_s)
    wait_bytes(gat.at[others], ag_s)
    gram_out[...] = gat[...]
    wait_bytes(result, out_sem)


def factor(u, out):
    sub = lax.broadcasted_iota(jnp.int32, (8, 128), 0)
    lane = lax.broadcasted_iota(jnp.int32, (8, 128), 1)
    zero = jnp.zeros((8, 128), jnp.float32)
    for b in range(32):
        r0 = 8 * b
        half, off = r0 // 128, r0 % 128
        halves = [0, 1] if half == 0 else [1]
        panel = {h: u[r0 : r0 + 8, 128 * h : 128 * h + 128] for h in halves}
        cols = [jnp.broadcast_to(panel[half][:, off + j : off + j + 1], (8, 128)) for j in range(8)]
        d = {
            (i, j): jnp.broadcast_to(cols[j][i : i + 1, :], (8, 128))
            for j in range(8)
            for i in range(j + 1)
        }
        rows = {h: [jnp.broadcast_to(panel[h][i : i + 1, :], (8, 128)) for i in range(8)] for h in halves}
        last = b == 31
        if not last:
            n0 = r0 + 8
            nhalf = n0 // 128
            nh = [0, 1] if nhalf == 0 else [1]
            following = {h: u[n0 : n0 + 8, 128 * h : 128 * h + 128] for h in nh}
            src = u[n0 : n0 + 8, 128 * half : 128 * half + 128]
            g = [jnp.broadcast_to(src[:, off + j : off + j + 1], (8, 128)) for j in range(8)]
        for j in range(8):
            scale = lax.rsqrt(d[j, j])
            for k in range(j + 1, 8):
                d[j, k] = d[j, k] * scale
            for h in halves:
                rows[h][j] = rows[h][j] * scale
            if not last:
                g[j] = g[j] * scale
                for h in nh:
                    following[h] = following[h] - g[j] * rows[h][j]
            for k in range(j + 1, 8):
                for l in range(k, 8):
                    d[k, l] = d[k, l] - d[j, k] * d[j, l]
                for h in halves:
                    rows[h][k] = rows[h][k] - d[j, k] * rows[h][j]
                if not last:
                    g[k] = g[k] - d[j, k] * g[j]
        done = {}
        for h in halves:
            x = rows[h][7]
            for i in range(7):
                x = jnp.where(sub == i, rows[h][i], x)
            done[h] = x
        for h in (0, 1):
            if h < half:
                value = zero
            elif h == half:
                value = jnp.where(lane >= off + sub, done[h], 0.0)
            else:
                value = done[h]
            out[r0 : r0 + 8, 128 * h : 128 * h + 128] = value
        if last:
            break
        for h in nh:
            u[n0 : n0 + 8, 128 * h : 128 * h + 128] = following[h]
        t0 = n0 + 8
        if t0 < 256:
            hs = [h for h in halves if h >= nhalf]
            parts = {h: split_of(done[h]) for h in hs}
            c0 = 128 * nhalf

            def stack(order):
                return jnp.concatenate(
                    [jnp.concatenate([parts[h][o] for h in hs], axis=1) for o in order], axis=0
                )

            left, right = stack([0, 0, 1, 1, 0, 2]), stack([0, 1, 0, 1, 2, 0])
            product = lax.dot_general(
                left[:, t0 - c0 :], right, (((0,), (0,)), ((), ())), preferred_element_type=jnp.float32
            )
            u[t0:256, c0:256] = u[t0:256, c0:256] - product


def factor_kernel(scale, gram, temp_hbm, next_hbm, triangle, u, sem):
    move = pltpu.make_async_copy(temp_hbm, next_hbm, sem)
    move.start()
    row = lax.broadcasted_iota(jnp.int32, (128, 128), 0)
    col = lax.broadcasted_iota(jnp.int32, (128, 128), 1)
    mixed = gram[0:16].reshape(128, 128) * scale
    cross = gram[16:32].reshape(128, 128) * scale
    diagonal = jnp.broadcast_to(gram[32, 0:1] * scale, (128, 128))
    turned = mixed.T
    u[0:128, 0:128] = jnp.where(col >= row, mixed, turned)
    u[128:256, 128:256] = jnp.where(col == row, diagonal, jnp.where(col < row, mixed, turned))
    u[0:128, 128:256] = cross
    u[128:256, 0:128] = cross.T
    factor(u, triangle)
    move.wait()


def local(n_gx, n_gy, section_start, section_now, history):
    fields, planes, cx, cy = section_now.shape
    older, samples = history.shape[:2]
    f32, bf16 = jnp.float32, jnp.bfloat16
    any_space = pl.BlockSpec(memory_space=pl.ANY)
    vmem = pl.BlockSpec(memory_space=pltpu.VMEM)
    section = jax.ShapeDtypeStruct(section_now.shape, f32)
    dma = pltpu.SemaphoreType.DMA
    tiles = n_gx + 1
    temp, gram = pl.pallas_call(
        functools.partial(section_kernel, n_gx, n_gy, planes),
        out_shape=(section, jax.ShapeDtypeStruct((tiles, 8, 128), f32)),
        in_specs=[any_space] * 4,
        out_specs=(any_space, vmem),
        scratch_shapes=[
            pltpu.VMEM(section_now.shape, f32),
            pltpu.VMEM(section_now.shape, f32),
            pltpu.VMEM(section_now.shape, f32),
            pltpu.VMEM((samples * cx // 2, older + 1, 2, cy), bf16),
            pltpu.VMEM((4, 2 * older + 2, 128), f32),
            pltpu.VMEM((2, fields, planes, 1, cy), f32),
            pltpu.VMEM((fields, cx, cy), f32),
            pltpu.VMEM((2, fields, cx, cy), f32),
            pltpu.VMEM((tiles, 8, 128), f32),
            pltpu.VMEM((n_gx, 8, 128), f32),
            pltpu.VMEM((n_gx, 8, 128), f32),
            pltpu.VMEM((n_gy, 2, 8, 128), f32),
            pltpu.VMEM((tiles, 8, 128), f32),
            dma, dma, dma((samples,)), dma,
            dma((2,)), dma((2,)), dma((2,)), dma((2,)),
        ] + [dma] * 10,
        compiler_params=pltpu.CompilerParams(
            collective_id=0, has_side_effects=True, vmem_limit_bytes=40 << 20
        ),
    )(
        section_now.reshape(fields, planes, cx, 1, cy),
        section_now,
        section_start,
        history.reshape(older, samples * cx // 2, 2, cy),
    )
    rows = samples * cx * cy * n_gx * n_gy
    return pl.pallas_call(
        functools.partial(factor_kernel, 1.0 / rows),
        out_shape=(section, jax.ShapeDtypeStruct((older + 1, older + 1), f32)),
        in_specs=[vmem, any_space],
        out_specs=(any_space, vmem),
        scratch_shapes=[pltpu.VMEM((older + 1, older + 1), f32), dma],
    )(gram, temp)


def solution(mesh):
    spec = P(None, None, "gx", "gy")
    return jax.shard_map(
        functools.partial(local, mesh.shape["gx"], mesh.shape["gy"]),
        mesh=mesh,
        in_specs=(spec, spec, spec),
        out_specs=(spec, P()),
        check_vma=False,
    )
```

profile of v0, /device:TPU:1, one launch (start us, length us, event | category | flops | bytes accessed | tf_op | source)
XLA Modules:
  0.0 105.1 jit_solution(10577886116528460520)
XLA Ops:
  0.6 0.0 copy-start
  0.6 3.4 %copy-done = bf16[255,16,8,128]{3,2,1,0:T(8,128)(2,1)S(1)} copy-done((bf16[255,16,8,128]{3,2,1,0:T(8,128)(2,1)S(1)}, bf16[255,16,8,128]{3,2,1,0:T(8,128)(2,1)}, u32[]{:S(2)}) %copy-start) | copy-done | bytes 8355864
  4.0 0.0 copy-start.1
  4.0 1.3 %copy-done.1 = f32[5,64,8,128]{3,2,1,0:T(8,128)S(1)} copy-done((f32[5,64,8,128]{3,2,1,0:T(8,128)S(1)}, f32[5,64,8,128]{3,2,1,0:T(8,128)}, u32[]{:S(2)}) %copy-start.1) | copy-done | bytes 1310744
  5.3 0.0 copy-start.2
  5.3 1.3 %copy-done.2 = f32[5,64,8,128]{3,2,1,0:T(8,128)S(1)} copy-done((f32[5,64,8,128]{3,2,1,0:T(8,128)S(1)}, f32[5,64,8,128]{3,2,1,0:T(8,128)}, u32[]{:S(2)}) %copy-start.2) | copy-done | bytes 1310744
  6.6 54.3 %shard_map.50 = (f32[5,64,8,128]{3,2,1,0:T(8,128)S(1)}, f32[33,8,128]{2,1,0:T(8,128)S(1)}) custom-call(f32[5,64,8,1,128]{4,3,2,1,0:T(1,128)S(1)} %bitcast.3, f32[5,64,8,128]{3,2,1,0:T(8,128)S(1)} %copy-done.1, f32[5,64,8,128]{3,2,1,0:T(8,128)S(1)} %copy-done.2, bf16[255,64,2,128]{3,2,1,0:T(2,128)(2,1)S(1)} %bitcast.2), custom_call_target="tpu_custom_call" | custom-call | tf_op jit(solution)/shard_map/pallas_call | solution.py:403
  61.0 0.0 copy-start.3
  61.0 1.1 %copy-done.3 = f32[5,64,8,128]{3,2,1,0:T(8,128)} copy-done((f32[5,64,8,128]{3,2,1,0:T(8,128)}, f32[5,64,8,128]{3,2,1,0:T(8,128)S(1)}, u32[]{:S(2)}) %copy-start.3) | copy-done | bytes 1310744
  62.0 0.0 copy-start.4
  62.0 0.6 copy-done.4
  62.7 42.4 %shard_map.51 = (f32[5,64,8,128]{3,2,1,0:T(8,128)}, f32[256,256]{1,0:T(8,128)}) custom-call(f32[33,8,128]{2,1,0:T(8,128)} %copy-done.4, f32[5,64,8,128]{3,2,1,0:T(8,128)} %copy-done.3), custom_call_target="tpu_custom_call" | custom-call | tf_op jit(solution)/shard_map/pallas_call | solution.py:435
Async XLA Ops:
  0.6 3.4 %copy-start = (bf16[255,16,8,128]{3,2,1,0:T(8,128)(2,1)S(1)}, bf16[255,16,8,128]{3,2,1,0:T(8,128)(2,1)}, u32[]{:S(2)}) copy-start(bf16[255,16,8,128]{3,2,1,0:T(8,128)(2,1)} %param.5) | copy-start | bytes 25067524
  4.0 1.3 %copy-start.1 = (f32[5,64,8,128]{3,2,1,0:T(8,128)S(1)}, f32[5,64,8,128]{3,2,1,0:T(8,128)}, u32[]{:S(2)}) copy-start(f32[5,64,8,128]{3,2,1,0:T(8,128)} %now_hbm.1) | copy-start | bytes 3932164
  5.3 1.3 %copy-start.2 = (f32[5,64,8,128]{3,2,1,0:T(8,128)S(1)}, f32[5,64,8,128]{3,2,1,0:T(8,128)}, u32[]{:S(2)}) copy-start(f32[5,64,8,128]{3,2,1,0:T(8,128)} %start_hbm.1) | copy-start | bytes 3932164
  61.0 1.1 %copy-start.3 = (f32[5,64,8,128]{3,2,1,0:T(8,128)}, f32[5,64,8,128]{3,2,1,0:T(8,128)S(1)}, u32[]{:S(2)}) copy-start(f32[5,64,8,128]{3,2,1,0:T(8,128)S(1)} %get-tuple-element.5.temp_hbm) | copy-start | bytes 3932164
  62.0 0.7 copy-start.4
where the time goes:
time: 105 us
  Pallas kernels  96.7 us (92%)
  local copies, waits for them, and re-layouts  7.71 us (7%)
    pallas_call x1, Pallas kernels, local(): pl.pallas_call(functools.partial(section_kernel, n_gx, n_gy, planes), out...  54.3 us
    pallas_call x1, Pallas kernels, local(): pl.pallas_call(functools.partial(factor_kernel, 1.0 / rows), out_shape=(s...  42.4 us
    unnamed x10, local copies, waits for them, and re-layouts  7.71 us

commit v1 on v0

v1 whole, which is shorter than its diff:
```python
import functools

import jax
import jax.numpy as jnp
from jax import lax
from jax.experimental import pallas as pl
from jax.experimental.pallas import tpu as pltpu
from jax.sharding import PartitionSpec as P

ZSUB = 4
LINE = 4
EARLY = 8
CUTS = (6, 10)
GAMMA_LESS = 0.4
TIME_STEP = 0.2
VISCOUS = 0.25
MESH = pl.DeviceIdType.MESH
FLUX = 0.25 * TIME_STEP * 0.5
NEAR = 0.25 * TIME_STEP * VISCOUS
OWN = 0.25 - 6.0 * NEAR


def wait_bytes(ref, sem):
    pltpu.make_async_copy(ref, ref, sem).wait()


def pressure_of(q, inverse):
    kinetic = q[1] * q[1] + q[2] * q[2] + q[3] * q[3]
    return GAMMA_LESS * (q[4] - 0.5 * kinetic * inverse)


def plane_of(q):
    inverse = 1.0 / q[0]
    pressure = pressure_of(q, inverse)
    return q, inverse * FLUX, pressure * FLUX, q[4] + pressure


def flux_of(plane, k, sign=None):
    q, scaled, pressure, enthalpy = plane
    if sign is not None:
        scaled, pressure = scaled * sign, pressure * sign
    velocity = q[k] * scaled
    flux = [q[0] * velocity]
    for member in (1, 2, 3):
        term = q[member] * velocity
        flux.append(term + pressure if member == k else term)
    flux.append(enthalpy * velocity)
    return flux


def both_of(plane, k):
    flux = flux_of(plane, k)
    base = [NEAR * value for value in plane[0]]
    return [b + f for b, f in zip(base, flux)], [b - f for b, f in zip(base, flux)]


def edge_of(q, k, sign):
    flux = flux_of(plane_of(q), k, sign)
    return [NEAR * value + f for value, f in zip(q, flux)]


def fold(acc, first, second):
    row = lax.broadcasted_iota(jnp.int32, (256, 128), 0)
    col = lax.broadcasted_iota(jnp.int32, (256, 128), 1)
    total = jnp.zeros((128, 128), jnp.float32)
    for parity in (0, 1):
        pick = (row == 2 * col + parity).astype(jnp.bfloat16)
        for h in (0, 1):
            part = acc[2 * second + h, pl.ds(256 * first + parity, 128, stride=2), :]
            chosen = pick[128 * h : 128 * h + 128]
            for piece in split_of(part):
                total = total + jnp.dot(piece, chosen, preferred_element_type=jnp.float32)
    return total


def split_of(x):
    high = x.astype(jnp.bfloat16)
    rest = x - high.astype(jnp.float32)
    middle = rest.astype(jnp.bfloat16)
    low = (rest - middle.astype(jnp.float32)).astype(jnp.bfloat16)
    return high, middle, low


def section_kernel(
    n_gx, n_gy, planes,
    rows_hbm, now_hbm, start_hbm, hist_hbm, next_hbm, gram_out,
    now, start, result, hist, acc, acc_new, xhalo, xrest, ysend, yhalo, yedge,
    packed, rs, rs_extra, ex, gat,
    now_sem, start_sem, hist_sem, out_sem,
    xs, xr, ys, yr, rs_s, rs_r, re_s, re_r, ex_s, ex_r, ag_s, ag_r, ae_s, ae_r,
):
    a, c = lax.axis_index("gx"), lax.axis_index("gy")
    n_z = n_gx // LINE
    zz, yy = a // LINE, lax.rem(a, LINE)
    n_near = LINE * n_gy
    me = yy * n_gy + c
    samples = planes // ZSUB
    pairs = hist_hbm.shape[1] // samples
    older = hist_hbm.shape[0]
    load_now = pltpu.make_async_copy(now_hbm, now, now_sem)
    load_start = pltpu.make_async_copy(start_hbm, start, start_sem)
    load_now.start()
    barrier = pltpu.get_barrier_semaphore()
    up, down = lax.rem(a + 1, n_gx), lax.rem(a + n_gx - 1, n_gx)
    ahead, behind = lax.rem(c + 1, n_gy), lax.rem(c + n_gy - 1, n_gy)

    def near_of(d):
        order = lax.rem(d, LINE)
        turn = d // LINE
        dy = jnp.where(order == 0, 2, jnp.where(order == 3, 0, 2 * order - 1))
        other = n_gy - 1 - turn
        dc = jnp.where(other < 2, other, jnp.where(other < 4, other + 4, other - 2))
        y = lax.rem(yy + dy, LINE)
        return y, lax.rem(c + dc, n_gy)

    def far_of(d):
        half = n_z // 2
        dz = jnp.where(lax.rem(d, 2) == 0, half + d // 2, half - 1 - d // 2)
        return lax.rem(zz + dz, n_z)

    def greet(where):
        pl.semaphore_signal(barrier, inc=1, device_id=where, device_id_type=MESH)

    def greet_near(d, carry):
        y, core = near_of(d)
        greet((zz * LINE + y, core))
        return carry

    def greet_far(d, carry):
        greet((far_of(d) * LINE + yy, c))
        return carry

    for where in ((up, c), (down, c), (a, ahead), (a, behind)):
        greet(where)
    lax.fori_loop(0, n_near - 1, greet_near, 0)
    lax.fori_loop(0, n_z - 1, greet_far, 0)

    def load_history(z, carry):
        for i in range(pairs):
            pltpu.make_async_copy(
                hist_hbm.at[:, z * pairs + i], hist.at[z * pairs + i, pl.ds(0, older)], hist_sem.at[z]
            ).start()
        return carry

    lax.fori_loop(0, samples // 2, load_history, 0)
    load_start.start()
    pl.semaphore_wait(barrier, n_near - 1 + n_z - 1 + 4)

    def to(src, dst, send, recv, where):
        return pltpu.make_async_remote_copy(
            src_ref=src, dst_ref=dst, send_sem=send, recv_sem=recv, device_id=where, device_id_type=MESH
        )

    halos = [
        to(rows_hbm.at[:, :, 0, 7], xhalo.at[0], xs.at[0], xr.at[0], (up, c)),
        to(rows_hbm.at[:, :, 0, 0], xhalo.at[1], xs.at[1], xr.at[1], (down, c)),
        to(ysend.at[0], yhalo.at[0, 0], ys.at[0], yr.at[0], (a, ahead)),
        to(ysend.at[0], yhalo.at[0, 1], ys.at[1], yr.at[1], (a, behind)),
    ]
    rest = [
        to(rows_hbm.at[:, :, pl.ds(1, ZSUB - 1), 7], xrest.at[0], xs.at[2], xr.at[2], (up, c)),
        to(rows_hbm.at[:, :, pl.ds(1, ZSUB - 1), 0], xrest.at[1], xs.at[3], xr.at[3], (down, c)),
        to(ysend.at[1], yhalo.at[1, 0], ys.at[2], yr.at[2], (a, ahead)),
        to(ysend.at[1], yhalo.at[1, 1], ys.at[3], yr.at[3], (a, behind)),
    ]
    halos[0].start()
    halos[1].start()
    lane = lax.broadcasted_iota(jnp.int32, (8, 128), 1)
    sub = lax.broadcasted_iota(jnp.int32, (8, 128), 0)
    zero = jnp.zeros((8, 128), jnp.float32)
    load_now.wait()

    def pack_edges(count, stride, where):
        def one(i, carry):
            mask = lax.rem(lane - 2 * i + 129, 128) < 2
            return tuple(
                jnp.where(mask, pltpu.roll(now[f, i * stride], 2 * i, 1), carry[f]) for f in range(5)
            )

        edges = lax.fori_loop(0, count, one, (zero,) * 5, unroll=4)
        for f in range(5):
            ysend[where, f] = edges[f]

    pack_edges(samples, ZSUB, 0)
    halos[2].start()
    halos[3].start()
    rest[0].start()
    rest[1].start()
    lax.fori_loop(samples // 2, samples, load_history, 0)
    pack_edges(planes, 1, 1)
    rest[2].start()
    rest[3].start()

    acc[...] = jnp.zeros_like(acc)
    acc_new[...] = jnp.zeros_like(acc_new)
    hist[pl.ds(0, EARLY * pairs), older] = jnp.zeros((EARLY * pairs, 2, 128), jnp.bfloat16)

    def block_of(s):
        return jnp.concatenate(
            [hist[s * pairs + i].reshape(2 * older + 2, 128) for i in range(pairs)], axis=1
        )

    def multiply(s):
        block = block_of(s)
        for i, j in ((0, 0), (0, 1), (1, 1)):
            rows, cols = slice(256 * i, 256 * i + 256), slice(256 * j, 256 * j + 256)
            product = lax.dot_general(
                block[rows], block[cols], (((1,), (1,)), ((), ())), preferred_element_type=jnp.float32
            )
            acc[2 * j, rows] += product[:, :128]
            acc[2 * j + 1, rows] += product[:, 128:]

    def wait_history(s):
        spot = pl.multiple_of(s * pairs, pairs)
        wait_bytes(hist.at[pl.ds(spot, pairs), pl.ds(0, older)], hist_sem.at[s])

    def early(s, carry):
        wait_history(s)
        multiply(s)
        return carry

    lax.fori_loop(0, EARLY, early, 0)
    load_start.wait()
    for copy in halos:
        copy.wait_recv()
    even = lax.rem(lane, 2) == 0

    def merge_edges(which):
        for f in range(5):
            yedge[which, f] = jnp.where(even, yhalo[which, 1, f], yhalo[which, 0, f])

    merge_edges(0)
    xsign = jnp.where(sub == 7, 1.0, -1.0)
    ysign = jnp.where(lane == 127, 1.0, -1.0)

    def load(z):
        return plane_of([now[f, z] for f in range(5)])

    def advance(z, plane, below, above, low, high, which, i):
        p1, n1 = both_of(plane, 1)
        p2, n2 = both_of(plane, 2)
        xe = edge_of([jnp.where(sub < 4, high[f], low[f]) for f in range(5)], 1, xsign)
        turn = lax.rem(128 - 2 * i, 128)
        yq = [pltpu.roll(yedge[which, f], turn, 1) for f in range(5)]
        yq[0] = jnp.where((lane == 0) | (lane == 127), yq[0], 1.0)
        ye = edge_of(yq, 2, ysign)
        fresh = []
        for f in range(5):
            total = below[f] + above[f]
            total += pltpu.roll(jnp.where(sub == 7, xe[f], p1[f]), 1, 0)
            total += pltpu.roll(jnp.where(sub == 0, xe[f], n1[f]), 7, 0)
            total += pltpu.roll(jnp.where(lane == 127, ye[f], p2[f]), 1, 1)
            total += pltpu.roll(jnp.where(lane == 0, ye[f], n2[f]), 127, 1)
            total += 0.75 * start[f, z] + OWN * plane[0][f]
            result[f, z] = total
            fresh.append(total)
        return fresh

    def sampled(s):
        z = s * ZSUB
        below = both_of(load(jnp.maximum(z - 1, 0)), 3)[0]
        above = both_of(load(z + 1), 3)[1]
        low, high = ([xhalo[side, f, s] for f in range(5)] for side in (0, 1))
        fresh = advance(z, load(z), below, above, low, high, 0, s)
        snapshot = pressure_of(fresh, 1.0 / fresh[0]).astype(jnp.bfloat16)
        hist[pl.ds(pl.multiple_of(s * pairs, pairs), pairs), older] = snapshot.reshape(pairs, 2, 128)

    def sample_two(i, carry):
        sampled(2 * i)
        sampled(2 * i + 1)
        return carry

    def late(s, carry):
        wait_history(s)
        multiply(s)
        return carry

    def newest(s, carry):
        block = block_of(s)
        acc_new[:, 0:16] += lax.dot_general(
            block, block[2 * older - 14 :], (((1,), (1,)), ((), ())), preferred_element_type=jnp.float32
        )
        return carry

    lax.fori_loop(0, samples // 2, sample_two, 0)
    lax.fori_loop(0, EARLY, newest, 0)
    lax.fori_loop(EARLY, samples, late, 0)

    row = lax.broadcasted_iota(jnp.int32, (128, 128), 0)
    col = lax.broadcasted_iota(jnp.int32, (128, 128), 1)

    def added(first):
        total = jnp.zeros((128, 128), jnp.float32)
        for parity in (0, 1):
            part = acc_new[pl.ds(256 * first + parity, 128, stride=2), :]
            total += jnp.broadcast_to(part[:, 14 + parity : 15 + parity], (128, 128))
        return jnp.where(col == 127, total, 0.0)

    g00 = fold(acc, 0, 0)
    g01 = fold(acc, 0, 1) + added(0)
    g11 = fold(acc, 1, 1) + added(1)
    mixed = jnp.where(col >= row, g11, g00)
    diagonal = jnp.sum(jnp.where(col == row, g00, 0.0), axis=0, keepdims=True)
    for t in range(16):
        packed[t] = mixed[8 * t : 8 * t + 8]
        packed[16 + t] = g01[8 * t : 8 * t + 8]
    packed[n_near] = jnp.broadcast_to(diagonal, (8, 128))

    def scatter(d, carry):
        y, core = near_of(d)
        to(packed.at[y * n_gy + core], rs.at[me], rs_s, rs_r, (zz * LINE + y, core)).start()
        return carry

    @pl.when(me != 0)
    def _():
        to(packed.at[n_near], rs_extra.at[me], re_s, re_r, (zz * LINE, 0)).start()

    lax.fori_loop(0, n_near - 1, scatter, 0, unroll=True)
    rs[me] = packed[me]
    for copy in rest:
        copy.wait_recv()
    merge_edges(1)

    def others(s, carry):
        z0 = s * ZSUB
        parts = [load(z0)]
        below = both_of(parts[0], 3)[0]
        here = load(z0 + 1)
        for k in range(1, ZSUB):
            z = z0 + k
            above = load(jnp.minimum(z + 1, planes - 1))
            low, high = ([xrest[side, f, s, k - 1] for f in range(5)] for side in (0, 1))
            advance(z, here, below, both_of(above, 3)[1], low, high, 1, z)
            below, here = both_of(here, 3)[0], above
        return carry

    def finish(first, last):
        lax.fori_loop(first, last, others, 0)
        part = pl.ds(first * ZSUB, (last - first) * ZSUB)
        pltpu.make_async_copy(result.at[:, part], next_hbm.at[:, part], out_sem).start()

    finish(0, CUTS[0])
    near_rest, far_rest = pl.ds(0, n_near - 1), pl.ds(0, n_z - 1)
    wait_bytes(rs.at[near_rest], rs_r)

    def total_of(ref, count):
        parts = [ref[i] for i in range(count)]
        while len(parts) > 1:
            parts = [sum(parts[i : i + 2]) for i in range(0, len(parts), 2)]
        return parts[0]

    ex[zz, 0] = total_of(rs, n_near)
    ex[zz, 1] = zero

    @pl.when(me == 0)
    def _():
        rs_extra[0] = packed[n_near]
        wait_bytes(rs_extra.at[near_rest], re_r)
        ex[zz, 1] = total_of(rs_extra, n_near)

    def exchange(d, carry):
        to(ex.at[zz], ex.at[zz], ex_s, ex_r, (far_of(d) * LINE + yy, c)).start()
        return carry

    lax.fori_loop(0, n_z - 1, exchange, 0, unroll=True)
    finish(CUTS[0], CUTS[1])
    wait_bytes(ex.at[far_rest], ex_r)
    whole = total_of(ex, n_z)
    gat[me] = whole[0]

    def spread(d, carry):
        y, core = near_of(d)
        to(gat.at[me], gat.at[me], ag_s, ag_r, (zz * LINE + y, core)).start()
        return carry

    @pl.when(me == 0)
    def _():
        gat[n_near] = whole[1]

        def spread_extra(d, carry):
            y, core = near_of(d)
            to(gat.at[n_near], gat.at[n_near], ae_s, ae_r, (zz * LINE + y, core)).start()
            return carry

        lax.fori_loop(0, n_near - 1, spread_extra, 0)

    lax.fori_loop(0, n_near - 1, spread, 0, unroll=True)
    finish(CUTS[1], samples)
    wait_bytes(gat.at[near_rest], ag_r)

    @pl.when(me != 0)
    def _():
        wait_bytes(gat.at[n_near], ae_r)
        wait_bytes(packed.at[n_near], re_s)

    @pl.when(me == 0)
    def _():
        wait_bytes(gat.at[near_rest], ae_s)

    gram_out[...] = gat[...]
    wait_bytes(rs.at[near_rest], rs_s)
    wait_bytes(ex.at[far_rest], ex_s)
    wait_bytes(gat.at[near_rest], ag_s)
    for copy in halos + rest:
        copy.wait_send()
    wait_bytes(result, out_sem)


def factor(u, out):
    sub = lax.broadcasted_iota(jnp.int32, (8, 128), 0)
    lane = lax.broadcasted_iota(jnp.int32, (8, 128), 1)
    zero = jnp.zeros((8, 128), jnp.float32)
    for b in range(32):
        r0 = 8 * b
        half, off = r0 // 128, r0 % 128
        halves = [0, 1] if half == 0 else [1]
        panel = {h: u[r0 : r0 + 8, 128 * h : 128 * h + 128] for h in halves}
        cols = [jnp.broadcast_to(panel[half][:, off + j : off + j + 1], (8, 128)) for j in range(8)]
        d = {
            (i, j): jnp.broadcast_to(cols[j][i : i + 1, :], (8, 128))
            for j in range(8)
            for i in range(j + 1)
        }
        rows = {h: [jnp.broadcast_to(panel[h][i : i + 1, :], (8, 128)) for i in range(8)] for h in halves}
        last = b == 31
        if not last:
            n0 = r0 + 8
            nhalf = n0 // 128
            nh = [0, 1] if nhalf == 0 else [1]
            following = {h: u[n0 : n0 + 8, 128 * h : 128 * h + 128] for h in nh}
            src = u[n0 : n0 + 8, 128 * half : 128 * half + 128]
            g = [jnp.broadcast_to(src[:, off + j : off + j + 1], (8, 128)) for j in range(8)]
        for j in range(8):
            scale = lax.rsqrt(d[j, j])
            for k in range(j + 1, 8):
                d[j, k] = d[j, k] * scale
            for h in halves:
                rows[h][j] = rows[h][j] * scale
            if not last:
                g[j] = g[j] * scale
                for h in nh:
                    following[h] = following[h] - g[j] * rows[h][j]
            for k in range(j + 1, 8):
                for l in range(k, 8):
                    d[k, l] = d[k, l] - d[j, k] * d[j, l]
                for h in halves:
                    rows[h][k] = rows[h][k] - d[j, k] * rows[h][j]
                if not last:
                    g[k] = g[k] - d[j, k] * g[j]
        done = {}
        for h in halves:
            x = rows[h][7]
            for i in range(7):
                x = jnp.where(sub == i, rows[h][i], x)
            done[h] = x
        for h in (0, 1):
            if h < half:
                value = zero
            elif h == half:
                value = jnp.where(lane >= off + sub, done[h], 0.0)
            else:
                value = done[h]
            out[r0 : r0 + 8, 128 * h : 128 * h + 128] = value
        if last:
            break
        for h in nh:
            u[n0 : n0 + 8, 128 * h : 128 * h + 128] = following[h]
        t0 = n0 + 8
        if t0 < 256:
            hs = [h for h in halves if h >= nhalf]
            parts = {h: split_of(done[h]) for h in hs}
            c0 = 128 * nhalf

            def stack(order):
                return jnp.concatenate(
                    [jnp.concatenate([parts[h][o] for h in hs], axis=1) for o in order], axis=0
                )

            left, right = stack([0, 0, 1, 1, 0, 2]), stack([0, 1, 0, 1, 2, 0])
            product = lax.dot_general(
                left[:, t0 - c0 :], right, (((0,), (0,)), ((), ())), preferred_element_type=jnp.float32
            )
            u[t0:256, c0:256] = u[t0:256, c0:256] - product


def factor_kernel(scale, gram, temp_hbm, next_hbm, triangle, u, held, in_sem, out_sem):
    take = pltpu.make_async_copy(temp_hbm, held, in_sem)
    give = pltpu.make_async_copy(held, next_hbm, out_sem)
    take.start()
    row = lax.broadcasted_iota(jnp.int32, (128, 128), 0)
    col = lax.broadcasted_iota(jnp.int32, (128, 128), 1)
    mixed = gram[0:16].reshape(128, 128) * scale
    cross = gram[16:32].reshape(128, 128) * scale
    diagonal = jnp.broadcast_to(gram[32, 0:1] * scale, (128, 128))
    turned = mixed.T
    u[0:128, 0:128] = jnp.where(col == row, diagonal, jnp.where(col < row, mixed, turned))
    u[128:256, 128:256] = jnp.where(col >= row, mixed, turned)
    u[0:128, 128:256] = cross
    u[128:256, 0:128] = cross.T
    take.wait()
    give.start()
    factor(u, triangle)
    give.wait()


def local(n_gx, n_gy, section_start, section_now, history):
    fields, planes, cx, cy = section_now.shape
    older, samples = history.shape[:2]
    f32, bf16 = jnp.float32, jnp.bfloat16
    any_space = pl.BlockSpec(memory_space=pl.ANY)
    vmem = pl.BlockSpec(memory_space=pltpu.VMEM)
    section = jax.ShapeDtypeStruct(section_now.shape, f32)
    dma = pltpu.SemaphoreType.DMA
    tiles = n_gx + 1
    temp, gram = pl.pallas_call(
        functools.partial(section_kernel, n_gx, n_gy, planes),
        out_shape=(section, jax.ShapeDtypeStruct((tiles, 8, 128), f32)),
        in_specs=[any_space] * 4,
        out_specs=(any_space, vmem),
        scratch_shapes=[
            pltpu.VMEM(section_now.shape, f32),
            pltpu.VMEM(section_now.shape, f32),
            pltpu.VMEM(section_now.shape, f32),
            pltpu.VMEM((samples * cx // 2, older + 1, 2, cy), bf16),
            pltpu.VMEM((4, 2 * older + 2, 128), f32),
            pltpu.VMEM((2 * older + 2, 128), f32),
            pltpu.VMEM((2, fields, samples, 1, cy), f32),
            pltpu.VMEM((2, fields, samples, ZSUB - 1, 1, cy), f32),
            pltpu.VMEM((2, fields, cx, cy), f32),
            pltpu.VMEM((2, 2, fields, cx, cy), f32),
            pltpu.VMEM((2, fields, cx, cy), f32),
            pltpu.VMEM((tiles, 8, 128), f32),
            pltpu.VMEM((n_gx, 8, 128), f32),
            pltpu.VMEM((n_gx, 8, 128), f32),
            pltpu.VMEM((n_gx // LINE, 2, 8, 128), f32),
            pltpu.VMEM((tiles, 8, 128), f32),
            dma, dma, dma((samples,)), dma,
            dma((4,)), dma((4,)), dma((4,)), dma((4,)),
        ] + [dma] * 10,
        compiler_params=pltpu.CompilerParams(
            collective_id=0, has_side_effects=True, vmem_limit_bytes=60 << 20
        ),
    )(
        section_now.reshape(fields, samples, ZSUB, cx, 1, cy),
        section_now,
        section_start,
        history.reshape(older, samples * cx // 2, 2, cy),
    )
    rows = samples * cx * cy * n_gx * n_gy
    return pl.pallas_call(
        functools.partial(factor_kernel, 1.0 / rows),
        out_shape=(section, jax.ShapeDtypeStruct((older + 1, older + 1), f32)),
        in_specs=[vmem, any_space],
        out_specs=(any_space, vmem),
        scratch_shapes=[
            pltpu.VMEM((older + 1, older + 1), f32),
            pltpu.VMEM(section_now.shape, f32),
            dma, dma,
        ],
    )(gram, temp)


def solution(mesh):
    spec = P(None, None, "gx", "gy")
    return jax.shard_map(
        functools.partial(local, mesh.shape["gx"], mesh.shape["gy"]),
        mesh=mesh,
        in_specs=(spec, spec, spec),
        out_specs=(spec, P()),
        check_vma=False,
    )
```

time: 105 us -> 53.2 us (0.51)
  Pallas kernels: 96.7 us -> 52.4 us
  local copies, waits for them, and re-layouts: 7.71 us -> 0 us
    pallas_call x1, Pallas kernels: 42.4 us -> 11.7 us  [local(): pl.pallas_call(functools.partial(factor_kernel, 1.0 / rows), out_shape=(s...]
    pallas_call x1, Pallas kernels: 54.3 us -> 40.7 us  [local(): pl.pallas_call(functools.partial(section_kernel, n_gx, n_gy, planes), out...]
    unnamed x10 -> x0, local copies, waits for them, and re-layouts: 7.71 us -> none
where the time goes in v1:
time: 53.2 us; the launch traced here: 53 us
  Pallas kernels  52.4 us (98%)
  between operations  0.64 us (1%)
    pallas_call x1, Pallas kernels, local(): pl.pallas_call(functools.partial(section_kernel, n_gx, n_gy, planes), out...  40.7 us
    pallas_call x1, Pallas kernels, local(): pl.pallas_call(functools.partial(factor_kernel, 1.0 / rows), out_shape=(s...  11.7 us

profile of v1, /device:TPU:1, one launch (start us, length us, event | category | flops | bytes accessed | tf_op | source)
XLA Modules:
  0.0 53.0 jit_solution(7071046268592956731)
XLA Ops:
  0.6 40.7 %shard_map.50 = (f32[5,64,8,128]{3,2,1,0:T(8,128)}, f32[33,8,128]{2,1,0:T(8,128)}) custom-call(f32[5,16,4,8,1,128]{5,4,3,2,1,0:T(1,128)} %bitcast.3, f32[5,64,8,128]{3,2,1,0:T(8,128)} %now_hbm.1, f32[5,64,8,128]{3,2,1,0:T(8,128)} %start_hbm.1, bf16[255,64,2,128]{3,2,1,0:T(2,128)(2,1)} %bitcast.2), custom_call_target="tpu_custom_call" | custom-call | tf_op jit(solution)/shard_map/pallas_call | solution.py:515
  41.3 11.7 %shard_map.51 = (f32[5,64,8,128]{3,2,1,0:T(8,128)}, f32[256,256]{1,0:T(8,128)}) custom-call(f32[33,8,128]{2,1,0:T(8,128)} %get-tuple-element.4.gram, f32[5,64,8,128]{3,2,1,0:T(8,128)} %get-tuple-element.5.temp_hbm), custom_call_target="tpu_custom_call" | custom-call | tf_op jit(solution)/shard_map/pallas_call | solution.py:550

commit v2 on v1

--- a/solution.py
+++ b/solution.py
@@ -9,7 +9,8 @@
 
 ZSUB = 4
 LINE = 4
-EARLY = 8
+GROUP = 4
+AHEAD = 3
 CUTS = (6, 10)
 GAMMA_LESS = 0.4
 TIME_STEP = 0.2
@@ -84,9 +85,9 @@
 def section_kernel(
     n_gx, n_gy, planes,
     rows_hbm, now_hbm, start_hbm, hist_hbm, next_hbm, gram_out,
-    now, start, result, hist, acc, acc_new, xhalo, xrest, ysend, yhalo, yedge,
+    now, start, result, hist, acc, xhalo, xrest, ysend, yhalo, yedge,
     packed, rs, rs_extra, ex, gat,
-    now_sem, start_sem, hist_sem, out_sem,
+    now_sem, start_sem, hist_sem, out_sem, gram_sem,
     xs, xr, ys, yr, rs_s, rs_r, re_s, re_r, ex_s, ex_r, ag_s, ag_r, ae_s, ae_r,
 ):
     a, c = lax.axis_index("gx"), lax.axis_index("gy")
@@ -192,16 +193,14 @@
     rest[3].start()
 
     acc[...] = jnp.zeros_like(acc)
-    acc_new[...] = jnp.zeros_like(acc_new)
-    hist[pl.ds(0, EARLY * pairs), older] = jnp.zeros((EARLY * pairs, 2, 128), jnp.bfloat16)
-
-    def block_of(s):
+
+    def block_of(s, count):
         return jnp.concatenate(
-            [hist[s * pairs + i].reshape(2 * older + 2, 128) for i in range(pairs)], axis=1
+            [hist[s * pairs + i].reshape(2 * older + 2, 128) for i in range(pairs * count)], axis=1
         )
 
-    def multiply(s):
-        block = block_of(s)
+    def multiply(s, count):
+        block = block_of(s, count)
         for i, j in ((0, 0), (0, 1), (1, 1)):
             rows, cols = slice(256 * i, 256 * i + 256), slice(256 * j, 256 * j + 256)
             product = lax.dot_general(
@@ -211,15 +210,8 @@
             acc[2 * j + 1, rows] += product[:, 128:]
 
     def wait_history(s):
-        spot = pl.multiple_of(s * pairs, pairs)
-        wait_bytes(hist.at[pl.ds(spot, pairs), pl.ds(0, older)], hist_sem.at[s])
-
-    def early(s, carry):
-        wait_history(s)
-        multiply(s)
-        return carry
-
-    lax.fori_loop(0, EARLY, early, 0)
+        wait_bytes(hist.at[pl.ds(s * pairs, pairs), pl.ds(0, older)], hist_sem.at[s])
+
     load_start.wait()
     for copy in halos:
         copy.wait_recv()
@@ -263,42 +255,27 @@
         low, high = ([xhalo[side, f, s] for f in range(5)] for side in (0, 1))
         fresh = advance(z, load(z), below, above, low, high, 0, s)
         snapshot = pressure_of(fresh, 1.0 / fresh[0]).astype(jnp.bfloat16)
-        hist[pl.ds(pl.multiple_of(s * pairs, pairs), pairs), older] = snapshot.reshape(pairs, 2, 128)
+        hist[pl.ds(s * pairs, pairs), older] = snapshot.reshape(pairs, 2, 128)
 
     def sample_two(i, carry):
         sampled(2 * i)
         sampled(2 * i + 1)
         return carry
 
-    def late(s, carry):
-        wait_history(s)
-        multiply(s)
-        return carry
-
-    def newest(s, carry):
-        block = block_of(s)
-        acc_new[:, 0:16] += lax.dot_general(
-            block, block[2 * older - 14 :], (((1,), (1,)), ((), ())), preferred_element_type=jnp.float32
-        )
-        return carry
-
-    lax.fori_loop(0, samples // 2, sample_two, 0)
-    lax.fori_loop(0, EARLY, newest, 0)
-    lax.fori_loop(EARLY, samples, late, 0)
+    lax.fori_loop(0, GROUP // 2, sample_two, 0)
+    for s in range(0, samples, GROUP):
+        for t in range(s, s + GROUP):
+            wait_history(t)
+        multiply(s, GROUP)
+        for t in range(s + GROUP, min(s + 2 * GROUP, samples)):
+            sampled(t)
 
     row = lax.broadcasted_iota(jnp.int32, (128, 128), 0)
     col = lax.broadcasted_iota(jnp.int32, (128, 128), 1)
 
-    def added(first):
-        total = jnp.zeros((128, 128), jnp.float32)
-        for parity in (0, 1):
-            part = acc_new[pl.ds(256 * first + parity, 128, stride=2), :]
-            total += jnp.broadcast_to(part[:, 14 + parity : 15 + parity], (128, 128))
-        return jnp.where(col == 127, total, 0.0)
-
     g00 = fold(acc, 0, 0)
-    g01 = fold(acc, 0, 1) + added(0)
-    g11 = fold(acc, 1, 1) + added(1)
+    g01 = fold(acc, 0, 1)
+    g11 = fold(acc, 1, 1)
     mixed = jnp.where(col >= row, g11, g00)
     diagonal = jnp.sum(jnp.where(col == row, g00, 0.0), axis=0, keepdims=True)
     for t in range(16):
@@ -391,19 +368,25 @@
     @pl.when(me != 0)
     def _():
         wait_bytes(gat.at[n_near], ae_r)
+
+    hand_on = pltpu.make_async_copy(gat, gram_out, gram_sem)
+    hand_on.start()
+
+    @pl.when(me != 0)
+    def _():
         wait_bytes(packed.at[n_near], re_s)
 
     @pl.when(me == 0)
     def _():
         wait_bytes(gat.at[near_rest], ae_s)
 
-    gram_out[...] = gat[...]
     wait_bytes(rs.at[near_rest], rs_s)
     wait_bytes(ex.at[far_rest], ex_s)
     wait_bytes(gat.at[near_rest], ag_s)
     for copy in halos + rest:
         copy.wait_send()
     wait_bytes(result, out_sem)
+    hand_on.wait()
 
 
 def factor(u, out):
@@ -422,31 +405,34 @@
             for i in range(j + 1)
         }
         rows = {h: [jnp.broadcast_to(panel[h][i : i + 1, :], (8, 128)) for i in range(8)] for h in halves}
-        last = b == 31
-        if not last:
-            n0 = r0 + 8
-            nhalf = n0 // 128
-            nh = [0, 1] if nhalf == 0 else [1]
-            following = {h: u[n0 : n0 + 8, 128 * h : 128 * h + 128] for h in nh}
-            src = u[n0 : n0 + 8, 128 * half : 128 * half + 128]
-            g = [jnp.broadcast_to(src[:, off + j : off + j + 1], (8, 128)) for j in range(8)]
+        chalf = (r0 + 8) // 128
+        nh = [h for h in halves if h >= chalf]
+        starts = [r0 + 8 * step for step in range(1, AHEAD + 1) if r0 + 8 * step < 256]
+        following = [{h: u[n0 : n0 + 8, 128 * h : 128 * h + 128] for h in nh} for n0 in starts]
+        g = [
+            [
+                jnp.broadcast_to(u[n0 : n0 + 8, 128 * half : 128 * half + 128][:, off + j : off + j + 1], (8, 128))
+                for j in range(8)
+            ]
+            for n0 in starts
+        ]
         for j in range(8):
             scale = lax.rsqrt(d[j, j])
             for k in range(j + 1, 8):
                 d[j, k] = d[j, k] * scale
             for h in halves:
                 rows[h][j] = rows[h][j] * scale
-            if not last:
-                g[j] = g[j] * scale
+            for ahead, values in zip(g, following):
+                ahead[j] = ahead[j] * scale
                 for h in nh:
-                    following[h] = following[h] - g[j] * rows[h][j]
+                    values[h] = values[h] - ahead[j] * rows[h][j]
             for k in range(j + 1, 8):
                 for l in range(k, 8):
                     d[k, l] = d[k, l] - d[j, k] * d[j, l]
                 for h in halves:
                     rows[h][k] = rows[h][k] - d[j, k] * rows[h][j]
-                if not last:
-                    g[k] = g[k] - d[j, k] * g[j]
+                for ahead in g:
+                    ahead[k] = ahead[k] - d[j, k] * ahead[j]
         done = {}
         for h in halves:
             x = rows[h][7]
@@ -461,19 +447,17 @@
             else:
                 value = done[h]
             out[r0 : r0 + 8, 128 * h : 128 * h + 128] = value
-        if last:
-            break
-        for h in nh:
-            u[n0 : n0 + 8, 128 * h : 128 * h + 128] = following[h]
-        t0 = n0 + 8
+        for n0, values in zip(starts, following):
+            for h in nh:
+                u[n0 : n0 + 8, 128 * h : 128 * h + 128] = values[h]
+        t0 = r0 + 8 + 8 * AHEAD
         if t0 < 256:
-            hs = [h for h in halves if h >= nhalf]
-            parts = {h: split_of(done[h]) for h in hs}
-            c0 = 128 * nhalf
+            parts = {h: split_of(done[h]) for h in nh}
+            c0 = 128 * chalf
 
             def stack(order):
                 return jnp.concatenate(
-                    [jnp.concatenate([parts[h][o] for h in hs], axis=1) for o in order], axis=0
+                    [jnp.concatenate([parts[h][o] for h in nh], axis=1) for o in order], axis=0
                 )
 
             left, right = stack([0, 0, 1, 1, 0, 2]), stack([0, 1, 0, 1, 2, 0])
@@ -516,14 +500,13 @@
         functools.partial(section_kernel, n_gx, n_gy, planes),
         out_shape=(section, jax.ShapeDtypeStruct((tiles, 8, 128), f32)),
         in_specs=[any_space] * 4,
-        out_specs=(any_space, vmem),
+        out_specs=(any_space, any_space),
         scratch_shapes=[
             pltpu.VMEM(section_now.shape, f32),
             pltpu.VMEM(section_now.shape, f32),
             pltpu.VMEM(section_now.shape, f32),
             pltpu.VMEM((samples * cx // 2, older + 1, 2, cy), bf16),
             pltpu.VMEM((4, 2 * older + 2, 128), f32),
-            pltpu.VMEM((2 * older + 2, 128), f32),
             pltpu.VMEM((2, fields, samples, 1, cy), f32),
             pltpu.VMEM((2, fields, samples, ZSUB - 1, 1, cy), f32),
             pltpu.VMEM((2, fields, cx, cy), f32),
@@ -534,7 +517,7 @@
             pltpu.VMEM((n_gx, 8, 128), f32),
             pltpu.VMEM((n_gx // LINE, 2, 8, 128), f32),
             pltpu.VMEM((tiles, 8, 128), f32),
-            dma, dma, dma((samples,)), dma,
+            dma, dma, dma((samples,)), dma, dma,
             dma((4,)), dma((4,)), dma((4,)), dma((4,)),
         ] + [dma] * 10,
         compiler_params=pltpu.CompilerParams(

time: 53.2 us -> 49.7 us (0.934)
  Pallas kernels: 52.4 us -> 48.8 us
    pallas_call x1, Pallas kernels: 40.7 us -> 38.1 us  [local(): pl.pallas_call(functools.partial(section_kernel, n_gx, n_gy, planes), out...]
    pallas_call x1, Pallas kernels: 11.7 us -> 10.7 us  [local(): pl.pallas_call(functools.partial(factor_kernel, 1.0 / rows), out_shape=(s...]
where the time goes in v2:
time: 49.7 us; the launch traced here: 49.6 us
  Pallas kernels  48.8 us (98%)
  between operations  0.8 us (2%)
    pallas_call x1, Pallas kernels, local(): pl.pallas_call(functools.partial(section_kernel, n_gx, n_gy, planes), out...  38.1 us
    pallas_call x1, Pallas kernels, local(): pl.pallas_call(functools.partial(factor_kernel, 1.0 / rows), out_shape=(s...  10.7 us

profile of v2, /device:TPU:1, one launch (start us, length us, event | category | flops | bytes accessed | tf_op | source)
XLA Modules:
  0.0 49.6 jit_solution(7760295111713079677)
XLA Ops:
  0.6 38.1 %shard_map.50 = (f32[5,64,8,128]{3,2,1,0:T(8,128)}, f32[33,8,128]{2,1,0:T(8,128)}) custom-call(f32[5,16,4,8,1,128]{5,4,3,2,1,0:T(1,128)} %bitcast.3, f32[5,64,8,128]{3,2,1,0:T(8,128)} %now_hbm.1, f32[5,64,8,128]{3,2,1,0:T(8,128)} %start_hbm.1, bf16[255,64,2,128]{3,2,1,0:T(2,128)(2,1)} %bitcast.2), custom_call_target="tpu_custom_call" | custom-call | tf_op jit(solution)/shard_map/pallas_call | solution.py:499
  38.8 10.7 %shard_map.51 = (f32[5,64,8,128]{3,2,1,0:T(8,128)}, f32[256,256]{1,0:T(8,128)}) custom-call(f32[33,8,128]{2,1,0:T(8,128)} %get-tuple-element.4.gram, f32[5,64,8,128]{3,2,1,0:T(8,128)} %get-tuple-element.5.temp_hbm), custom_call_target="tpu_custom_call" | custom-call | tf_op jit(solution)/shard_map/pallas_call | solution.py:533

commit v3 on v2

--- a/solution.py
+++ b/solution.py
@@ -143,9 +143,8 @@
             ).start()
         return carry
 
-    lax.fori_loop(0, samples // 2, load_history, 0)
+    lax.fori_loop(0, samples, load_history, 0)
     load_start.start()
-    pl.semaphore_wait(barrier, n_near - 1 + n_z - 1 + 4)
 
     def to(src, dst, send, recv, where):
         return pltpu.make_async_remote_copy(
@@ -164,8 +163,6 @@
         to(ysend.at[1], yhalo.at[1, 0], ys.at[2], yr.at[2], (a, ahead)),
         to(ysend.at[1], yhalo.at[1, 1], ys.at[3], yr.at[3], (a, behind)),
     ]
-    halos[0].start()
-    halos[1].start()
     lane = lax.broadcasted_iota(jnp.int32, (8, 128), 1)
     sub = lax.broadcasted_iota(jnp.int32, (8, 128), 0)
     zero = jnp.zeros((8, 128), jnp.float32)
@@ -183,16 +180,11 @@
             ysend[where, f] = edges[f]
 
     pack_edges(samples, ZSUB, 0)
-    halos[2].start()
-    halos[3].start()
-    rest[0].start()
-    rest[1].start()
-    lax.fori_loop(samples // 2, samples, load_history, 0)
     pack_edges(planes, 1, 1)
-    rest[2].start()
-    rest[3].start()
-
     acc[...] = jnp.zeros_like(acc)
+    pl.semaphore_wait(barrier, n_near - 1 + n_z - 1 + 4)
+    for copy in halos:
+        copy.start()
 
     def block_of(s, count):
         return jnp.concatenate(
@@ -215,6 +207,8 @@
     load_start.wait()
     for copy in halos:
         copy.wait_recv()
+    for copy in rest:
+        copy.start()
     even = lax.rem(lane, 2) == 0
 
     def merge_edges(which):

time: 49.7 us -> 49.3 us (level)
  Pallas kernels: 48.8 us -> 48.3 us
where the time goes in v3:
time: 49.3 us; the launch traced here: 49.1 us
  Pallas kernels  48.3 us (98%)
  between operations  0.8 us (2%)
    pallas_call x1, Pallas kernels, local(): pl.pallas_call(functools.partial(section_kernel, n_gx, n_gy, planes), out...  37.7 us
    pallas_call x1, Pallas kernels, local(): pl.pallas_call(functools.partial(factor_kernel, 1.0 / rows), out_shape=(s...  10.7 us

profile of v3, /device:TPU:1, one launch (start us, length us, event | category | flops | bytes accessed | tf_op | source)
XLA Modules:
  0.0 49.1 jit_solution(8917075873306242193)
XLA Ops:
  0.6 37.7 %shard_map.50 = (f32[5,64,8,128]{3,2,1,0:T(8,128)}, f32[33,8,128]{2,1,0:T(8,128)}) custom-call(f32[5,16,4,8,1,128]{5,4,3,2,1,0:T(1,128)} %bitcast.3, f32[5,64,8,128]{3,2,1,0:T(8,128)} %now_hbm.1, f32[5,64,8,128]{3,2,1,0:T(8,128)} %start_hbm.1, bf16[255,64,2,128]{3,2,1,0:T(2,128)(2,1)} %bitcast.2), custom_call_target="tpu_custom_call" | custom-call | tf_op jit(solution)/shard_map/pallas_call | solution.py:493
  38.3 10.7 %shard_map.51 = (f32[5,64,8,128]{3,2,1,0:T(8,128)}, f32[256,256]{1,0:T(8,128)}) custom-call(f32[33,8,128]{2,1,0:T(8,128)} %get-tuple-element.4.gram, f32[5,64,8,128]{3,2,1,0:T(8,128)} %get-tuple-element.5.temp_hbm), custom_call_target="tpu_custom_call" | custom-call | tf_op jit(solution)/shard_map/pallas_call | solution.py:527
